TPU v7x, 32 devices: a whole 2x2x4 slice. The times are simulated.
32 devices in a mesh: dp: 8 (over z, y), head: 4 (over x, core).
Axes of the slice: x: 2, y: 2, z: 4, core: 2. Of those that a mesh axis runs over, the one named last changes fastest.
Arguments:
- hidden_in: bfloat16 [2048, 2048], P(('dp', 'head')), may hold values from -6 to 6
- norm_gain: bfloat16 [2048], replicated, may hold values from 0.25 to 1.75
- w_query: bfloat16 [2048, 2048], P(None, 'head'), may hold values from -0.125 to 0.125
- key_weight: bfloat16 [2048, 1024], P(None, 'head'), may hold values from -0.125 to 0.125
- w_value: bfloat16 [2048, 1024], P(None, 'head'), may hold values from -0.125 to 0.125
- query_gain: bfloat16 [128], replicated, may hold values from 0.796875 to 4
- key_gain: bfloat16 [128], replicated, may hold values from 0.25 to 1.75
- w_out: bfloat16 [2048, 2048], P('head'), may hold values from -0.125 to 0.125
- prefix_root_keys: bfloat16 [1024, 1024], P('dp', 'head'), may hold values from -210 to 210
- prefix_root_values: bfloat16 [1024, 1024], P('dp', 'head'), may hold values from -6 to 6
- mid_keys: bfloat16 [4096, 1024], P('dp', 'head'), may hold values from -210 to 210
- mid_values: bfloat16 [4096, 1024], P('dp', 'head'), may hold values from -6 to 6
- mid_lengths: int32 [16], replicated, may hold values from 1 to 256, 2048 in all
- leaf_keys: bfloat16 [4096, 1024], P('dp', 'head'), may hold values from -6 to 6
- leaf_values: bfloat16 [4096, 1024], P('dp', 'head'), may hold values from -6 to 6
- leaf_lengths: int32 [64], P('dp'), may hold values from 1 to 64, 2048 in all
- token_request: int32 [8, 256], P('dp'), may hold values from 0 to 7, never falling along the last dimension, each value on 1 to 64 neighbouring positions
- request_node: int32 [8, 8], P('dp'), may hold values from 0 to 15, as said below
Outputs:
- attn_update: bfloat16 [2048, 2048], P(('dp', 'head'))
- cache_keys: bfloat16 [2048, 1024], P('dp', 'head')
- cache_values: bfloat16 [2048, 1024], P('dp', 'head')
Inputs may be any that keep to these rules, and one draw needn't show every extreme that they name: `token_request`: in each row requests 0 to 7 all occur, in rising order, each on 1 to 64 consecutive tokens; some request has exactly 64. `request_node`: node v is held by dp index v // 2; the 8 requests of one row have parents on 8 different dp indices, one each.
All inputs are finite; a program needn't handle non-finite values. No bound on the sum of `leaf_lengths` on one device may be relied on, other than what follows from the above.
Results may differ from a plain program's by a relative error of at most 0.039.
Values may be sent and summed in bfloat16 or wider, within the bound.
A program may use at most 128 MiB of HBM per device.

v0:
```python
import math
import jax
import jax.numpy as jnp
from jax import lax
from jax.sharding import PartitionSpec as P

MID_DEV = 2
MID_LEN = 256
EPS = 1e-06
THETA = 1000000.0
MASKED = -1e30


def rms_rows(values, gain):
    power = jnp.mean(values * values, axis=-1, keepdims=True)
    return values * lax.rsqrt(power + EPS) * gain


def rotate(values, positions):
    width = values.shape[-1]
    half = width // 2
    exponent = jnp.arange(half).astype(jnp.float32) * (2.0 / width)
    freqs = jnp.power(THETA, -exponent)
    angles = positions.astype(jnp.float32)[:, None] * freqs[None, :]
    cosine = jnp.cos(angles)[:, None, :]
    sine = jnp.sin(angles)[:, None, :]
    first = values[..., :half]
    second = values[..., half:]
    return jnp.concatenate(
        [first * cosine - second * sine, second * cosine + first * sine], axis=-1
    )


def body(
    hidden_in,
    norm_gain,
    w_query,
    key_weight,
    w_value,
    query_gain,
    key_gain,
    w_out,
    prefix_root_keys,
    prefix_root_values,
    mid_keys,
    mid_values,
    mid_lengths,
    leaf_keys,
    leaf_values,
    leaf_lengths,
    token_request,
    request_node,
):
    head_dim = query_gain.shape[0]
    query_width = w_query.shape[1]
    key_width = key_weight.shape[1]
    kv_heads = key_width // head_dim
    query_group = query_width // key_width
    scale = 1.0 / math.sqrt(head_dim)
    dp_count = lax.axis_size("dp")
    normalized_input = rms_rows(
        hidden_in.astype(jnp.float32), norm_gain.astype(jnp.float32)
    ).astype(jnp.bfloat16)
    piece = lax.all_gather(normalized_input, "head", axis=0, tiled=True)
    mixed = jnp.concatenate(
        [
            jnp.dot(piece, w_query, preferred_element_type=jnp.float32),
            jnp.dot(piece, key_weight, preferred_element_type=jnp.float32),
            jnp.dot(piece, w_value, preferred_element_type=jnp.float32),
        ],
        axis=1,
    )
    height = mixed.shape[0]
    segment = token_request[0]
    branch_nodes = request_node[0]
    requests = branch_nodes.shape[0]
    request_ids = jnp.arange(requests, dtype=jnp.int32)
    token_ids = jnp.arange(height, dtype=jnp.int32)
    member = segment[None, :] == request_ids[:, None]
    counts = jnp.sum(member.astype(jnp.int32), axis=1)
    earlier = request_ids[None, :] < request_ids[:, None]
    starts = jnp.sum(jnp.where(earlier, counts[None, :], 0), axis=1)
    offset = token_ids - jnp.sum(jnp.where(member, starts[:, None], 0), axis=0)
    node_total = mid_lengths.shape[0]
    node_match = branch_nodes[:, None] == jnp.arange(node_total, dtype=jnp.int32)[None, :]
    branch_length = jnp.sum(jnp.where(node_match, mid_lengths[None, :], 0), axis=1)
    root_total = prefix_root_keys.shape[0] * dp_count
    positions = (
        root_total
        + jnp.sum(jnp.where(member, (branch_length + leaf_lengths)[:, None], 0), axis=0)
        + offset
    )
    query_part = mixed[:, :query_width].reshape(height, query_width // head_dim, head_dim)
    key_portion = mixed[:, query_width : query_width + key_width].reshape(
        height, kv_heads, head_dim
    )
    query_matrix = rotate(rms_rows(query_part, query_gain.astype(jnp.float32)), positions).astype(
        jnp.bfloat16
    )
    new_keys = rotate(rms_rows(key_portion, key_gain.astype(jnp.float32)), positions).astype(
        jnp.bfloat16
    )
    new_values = mixed[:, query_width + key_width :].astype(jnp.bfloat16)
    heads_query = query_matrix.reshape(height, kv_heads, query_group, head_dim)
    root_keys = lax.all_gather(prefix_root_keys, "dp", axis=0, tiled=True)
    root_values = lax.all_gather(prefix_root_values, "dp", axis=0, tiled=True)
    owner_of = branch_nodes // MID_DEV
    owner_ids = jnp.arange(dp_count, dtype=jnp.int32)
    owner_match = owner_of[None, :] == owner_ids[:, None]
    block_slot = jnp.sum(jnp.where(owner_match, (branch_nodes % MID_DEV)[None, :], 0), axis=1)
    block_request = jnp.sum(jnp.where(owner_match, request_ids[None, :], 0), axis=1)
    block_length = jnp.sum(jnp.where(owner_match, branch_length[None, :], 0), axis=1)
    wanted = lax.all_to_all(block_slot[:, None], "dp", split_axis=0, concat_axis=0, tiled=True)[
        :, 0
    ]
    second = (wanted == 1)[:, None, None]
    own_pairs = jnp.concatenate([mid_keys, mid_values], axis=1).reshape(
        MID_DEV, MID_LEN, 2 * key_width
    )
    sent = jnp.where(second, own_pairs[1][None], own_pairs[0][None])
    got = lax.all_to_all(sent, "dp", split_axis=0, concat_axis=0, tiled=True)
    got = got.reshape(dp_count * MID_LEN, 2 * key_width)
    leaf_each = leaf_keys.shape[0] // requests
    leaf_live = jnp.arange(leaf_each, dtype=jnp.int32)[None, :] < leaf_lengths[:, None]
    leaf_tag = jnp.where(leaf_live, request_ids[:, None], -1).reshape(-1)
    mid_live = jnp.arange(MID_LEN, dtype=jnp.int32)[None, :] < block_length[:, None]
    mid_tag = jnp.where(mid_live, block_request[:, None], -1).reshape(-1)
    own_mask = (segment[None, :] == segment[:, None]) & (token_ids[None, :] <= token_ids[:, None])
    mask = jnp.concatenate(
        [
            jnp.ones((height, root_keys.shape[0]), jnp.bool_),
            leaf_tag[None, :] == segment[:, None],
            own_mask,
            mid_tag[None, :] == segment[:, None],
        ],
        axis=1,
    )
    all_keys = jnp.concatenate(
        [root_keys, leaf_keys, new_keys.reshape(height, key_width), got[:, :key_width]], axis=0
    ).reshape(-1, kv_heads, head_dim)
    all_values = jnp.concatenate(
        [root_values, leaf_values, new_values, got[:, key_width:]], axis=0
    ).reshape(-1, kv_heads, head_dim)
    scores = jnp.einsum("tkgd,skd->kgts", heads_query, all_keys, preferred_element_type=jnp.float32)
    scores = jnp.where(mask[None, None], scores * scale, MASKED)
    weights = jnp.exp(scores - jnp.max(scores, axis=-1, keepdims=True))
    total = jnp.sum(weights, axis=-1)
    summed = jnp.einsum(
        "kgts,skd->kgtd",
        weights.astype(jnp.bfloat16),
        all_values,
        preferred_element_type=jnp.float32,
    )
    attn = (summed / total[..., None]).astype(jnp.bfloat16)
    attn = attn.transpose(2, 0, 1, 3).reshape(height, query_width)
    update = lax.psum_scatter(
        jnp.dot(attn, w_out, preferred_element_type=jnp.float32).astype(jnp.bfloat16),
        "head",
        scatter_dimension=0,
        tiled=True,
    )
    return (update, new_keys.reshape(height, key_width), new_values)


def solution(mesh):
    in_specs = (
        P(("dp", "head"), None),
        P(),
        P(None, "head"),
        P(None, "head"),
        P(None, "head"),
        P(),
        P(),
        P("head", None),
        P("dp", "head"),
        P("dp", "head"),
        P("dp", "head"),
        P("dp", "head"),
        P(),
        P("dp", "head"),
        P("dp", "head"),
        P("dp"),
        P("dp", None),
        P("dp", None),
    )
    out_specs = (P(("dp", "head"), None), P("dp", "head"), P("dp", "head"))
    return jax.shard_map(body, mesh=mesh, in_specs=in_specs, out_specs=out_specs, check_vma=False)
```

profile of v0, /device:TPU:0, one launch (start us, length us, event | category | flops | bytes accessed | tf_op | source)
XLA Modules:
  0.0 206.7 jit_solution(16049318135466380190)
XLA Ops:
  9.7 7.3 %all-to-all-start = ((s32[8,1,1]{2,1,0:T(1,128)}), s32[8,1,1]{2,1,0:T(1,128)S(1)}, u32[]{:S(2)}, u32[]{:S(2)}) async-start(s32[8,1,1]{2,1,0:T(1,128)} %copy.122), calls=%async_computation | async-start | bytes 8192 | tf_op jit(solution)/shard_map/all_to_all | solution.py:113
  18.8 1.8 fusion.24
  25.8 29.8 %all_gather.11 = bf16[1024,256]{0,1:T(8,128)(2,1)} all-gather(bf16[128,256]{0,1:T(8,128)(2,1)S(1)} %copy.133), channel_id=1, replica_groups=mesh['dp'=8,'head'=4] {'dp'}, dimensions={0}, use_global_device_ids=true | all-gather | bytes 589824 | tf_op jit(solution)/shard_map/all_gather | solution.py:106
  56.5 27.1 %all_gather.9 = bf16[1024,256]{0,1:T(8,128)(2,1)S(1)} all-gather(bf16[128,256]{0,1:T(8,128)(2,1)S(1)} %copy.119), channel_id=1, replica_groups=mesh['dp'=8,'head'=4] {'dp'}, dimensions={0}, use_global_device_ids=true | all-gather | bytes 589824 | tf_op jit(solution)/shard_map/all_gather | solution.py:105
  84.4 1.8 copy.124
  86.2 1.8 copy.123
  88.0 1.8 copy.134
  91.1 1.8 copy.120
  92.9 1.8 copy.127
  96.0 2.7 %broadcast_select_fusion = bf16[8,256,512]{1,2,0:T(8,128)(2,1)} fusion(pred[8]{0:T(512)(128)(4,1)S(1)} %compare_reduce_fusion, bf16[256,512]{0,1:T(8,128)(2,1)} %copy.124, bf16[256,512]{0,1:T(8,128)(2,1)} %copy.123), kind=kLoop, calls=%fused_computation.9 | loop fusion | flops 1048576 | bytes 2621448 | tf_op jit(solution)/shard_map/jit(_where)/select_n | solution.py:120
  98.6 4.4 %all-to-all-start.1 = ((bf16[8,256,512]{1,2,0:T(8,128)(2,1)}), bf16[8,256,512]{1,2,0:T(8,128)(2,1)}, u32[]{:S(2)}, u32[]{:S(2)}) async-start(bf16[8,256,512]{1,2,0:T(8,128)(2,1)} %broadcast_select_fusion), calls=%async_computation.1 | async-start | bytes 4194304 | tf_op jit(solution)/shard_map/all_to_all | solution.py:121
  103.2 7.0 %pad_add_fusion = pred[256,3840]{0,1:T(8,128)(4,1)} fusion(pred[256,2048]{0,1:T(8,128)(4,1)S(1)} %broadcast_compare_fusion, pred[256,256]{0,1:T(8,128)(4,1)S(1)} %fusion.28, pred[256,512]{0,1:T(8,128)(4,1)S(1)} %broadcast_compare_fusion.1, pred[3840]{0:T(1024)(128)(4,1)S(1)} %pad.8.clone), kind=kLoop, calls=%fused_computation.7 | loop fusion | flops 2949120 | bytes 1707776 | tf_op jit(solution)/shard_map/concatenate | solution.py:129
  110.2 2.0 convolution_convert_fusion.1
  112.9 2.6 %fusion.36 = f32[256,512]{1,0:T(8,128)S(1)} fusion(bf16[256,2048]{1,0:T(8,128)(2,1)} %all-gather.2.cloned.1.call-done, bf16[2048,512]{1,0:T(8,128)(2,1)} %param.20), kind=kOutput, calls=%fused_computation.82 | convolution fusion | flops 536870912 | bytes 3670016 | tf_op jit(solution)/shard_map/dot_general | solution.py:67
  119.6 22.3 %all-to-all-done.1 = bf16[8,256,512]{1,2,0:T(8,128)(2,1)} async-done(((bf16[8,256,512]{1,2,0:T(8,128)(2,1)}), bf16[8,256,512]{1,2,0:T(8,128)(2,1)}, u32[]{:S(2)}, u32[]{:S(2)}) %all-to-all-start.1) | async-done | bytes 2097184 | tf_op jit(solution)/shard_map/all_to_all | solution.py:121
  141.9 1.9 copy.142
  143.8 1.1 fusion.34
  145.0 1.3 copy.128
  146.3 10.1 %fusion.2 = (f32[2,2,256]{2,1,0:T(2,128)S(1)}, f32[2,3840,256,2]{2,1,3,0:T(8,128)}) fusion(pred[256,3840]{0,1:T(8,128)(4,1)} %pad_add_fusion, bf16[256,2,2,64]{3,0,2,1:T(8,128)(2,1)} %bitcast.71, bf16[256,2,2,64]{3,0,2,1:T(8,128)(2,1)} %bitcast.72, bf16[2048,2,128]{2,0,1:T(8,128)(2,1)} %copy.128, bf16[256,2,128]{2,0,1:T(8,128)(2,1)S(1)} %maximum_convert_fusion, ...), kind=kOutput, calls=%fused_computation.4 | convolution fusion | flops 1026817024 | bytes 18944000 | tf_op jit(solution)/shard_map/tkgd,skd->kgts/dot_general | solution.py:144
  156.4 9.1 %fusion = f32[2,2,256]{2,1,0:T(2,128)S(1)} fusion(f32[2,3840,256,2]{2,1,3,0:T(8,128)} %get-tuple-element.41, f32[2,2,256]{2,1,0:T(2,128)S(1)} %get-tuple-element.40, pred[256,3840]{0,1:T(8,128)(4,1)} %pad_add_fusion), kind=kLoop, calls=%fused_computation.2 | loop fusion | flops 15727616 | bytes 16719872 | tf_op jit(solution)/shard_map/reduce_sum | solution.py:147
  165.5 1.2 pad_maximum_fusion
  166.8 7.7 %fusion.19 = bf16[256,2,2,128]{0,3,2,1:T(8,128)(2,1)S(1)} fusion(bf16[3840,2,128,1]{0,2,3,1:T(8,128)(2,1)S(1)} %bitcast.67, f32[2,3840,256,2]{2,1,3,0:T(8,128)} %get-tuple-element.41, f32[2,2,256]{2,1,0:T(2,128)S(1)} %get-tuple-element.40, pred[256,3840]{0,1:T(8,128)(4,1)S(1)} %copy-done.3, f32[256,2,2]{0,2,1:T(2,128)S(1)} %bitcast.80), kind=kOutput, calls=%fused_computation.22 | convolution fusion | flops 1022623744 | bytes 18948096 | tf_op jit(solution)/shard_map/kgts,skd->kgtd/dot_general | solution.py:148
  174.5 1.7 convolution_convert_fusion
  177.2 22.7 %reduce-scatter.2.cloned.1.call-done = bf16[64,2048]{1,0:T(8,128)(2,1)} async-done(((bf16[256,2048]{1,0:T(8,128)(2,1)}), bf16[64,2048]{1,0:T(8,128)(2,1)}) %reduce-scatter.2.cloned.1.call-update) | async-done | bytes 262160 | tf_op jit(solution)/shard_map/reduce_scatter | solution.py:156
  (80 shorter events, 19.7 us)
Async XLA Ops:
  7.2 167.4 %copy-start = (bf16[512,2048]{1,0:T(8,128)(2,1)S(1)}, bf16[512,2048]{1,0:T(8,128)(2,1)}, u32[]{:S(2)}) copy-start(bf16[512,2048]{1,0:T(8,128)(2,1)} %param.25) | copy-start | bytes 6291460
  7.2 48.5 %copy-start.12 = (s32[1,256]{1,0:T(1,128)S(1)}, s32[1,256]{1,0:T(1,128)}, u32[]{:S(2)}) copy-start(s32[1,256]{1,0:T(1,128)} %param.34) | copy-start | bytes 3076
  7.2 49.2 %copy-start.11 = (bf16[128,256]{1,0:T(8,128)(2,1)S(1)}, bf16[128,256]{1,0:T(8,128)(2,1)}, u32[]{:S(2)}) copy-start(bf16[128,256]{1,0:T(8,128)(2,1)} %param.26) | copy-start | bytes 196612
  9.7 86.0 %all-to-all-start = ((s32[8,1,1]{2,1,0:T(1,128)}), s32[8,1,1]{2,1,0:T(1,128)S(1)}, u32[]{:S(2)}, u32[]{:S(2)}) async-start(s32[8,1,1]{2,1,0:T(1,128)} %copy.122), calls=%async_computation | async-start | bytes 8192 | tf_op jit(solution)/shard_map/all_to_all | solution.py:113
  17.0 93.2 %all-gather.2.cloned.1.call-start = ((), (), s32[]{:S(2)}) async-start(), calls=%async_computation.3 | async-start | bytes 1310720 | tf_op jit(solution)/shard_map/all_gather | solution.py:64
  98.6 43.3 %all-to-all-start.1 = ((bf16[8,256,512]{1,2,0:T(8,128)(2,1)}), bf16[8,256,512]{1,2,0:T(8,128)(2,1)}, u32[]{:S(2)}, u32[]{:S(2)}) async-start(bf16[8,256,512]{1,2,0:T(8,128)(2,1)} %broadcast_select_fusion), calls=%async_computation.1 | async-start | bytes 4194304 | tf_op jit(solution)/shard_map/all_to_all | solution.py:121
  103.0 96.9 %reduce-scatter.2.cloned.1.call-start = ((), (), s32[]{:S(2)}) async-start(), calls=%async_computation.4 | async-start | bytes 1310720 | tf_op jit(solution)/shard_map/reduce_scatter | solution.py:156
  112.1 4.9 %copy-start.6 = (bf16[256,256]{1,0:T(8,128)(2,1)}, bf16[256,256]{1,0:T(8,128)(2,1)S(1)}, u32[]{:S(2)}) copy-start(bf16[256,256]{1,0:T(8,128)(2,1)S(1)} %convolution_convert_fusion.1) | copy-start | bytes 393220
  115.7 2.8 %copy-start.1 = (bf16[256,2048]{1,0:T(8,128)(2,1)S(1)}, bf16[256,2048]{1,0:T(8,128)(2,1)}, u32[]{:S(2)}) copy-start(bf16[256,2048]{1,0:T(8,128)(2,1)} %all-gather.2.cloned.1.call-done) | copy-start | bytes 3145732
  115.7 2.8 %copy-start.4 = (bf16[2048,256]{1,0:T(8,128)(2,1)S(1)}, bf16[2048,256]{1,0:T(8,128)(2,1)}, u32[]{:S(2)}) copy-start(bf16[2048,256]{1,0:T(8,128)(2,1)} %param.21) | copy-start | bytes 3145732
  119.6 26.7 %copy-start.8 = (bf16[256,2,128]{2,0,1:T(8,128)(2,1)}, bf16[256,2,128]{2,0,1:T(8,128)(2,1)S(1)}, u32[]{:S(2)}) copy-start(bf16[256,2,128]{2,0,1:T(8,128)(2,1)S(1)} %maximum_convert_fusion) | copy-start | bytes 393220
  143.8 2.5 %copy-start.10 = (bf16[512,2,128]{2,0,1:T(8,128)(2,1)S(1)}, bf16[512,2,128]{2,0,1:T(8,128)(2,1)}, u32[]{:S(2)}) copy-start(bf16[512,2,128]{2,0,1:T(8,128)(2,1)} %copy.127) | copy-start | bytes 786436
  156.3 9.1 %copy-start.2 = (bf16[2048,256]{0,1:T(8,128)(2,1)S(1)}, bf16[2048,256]{0,1:T(8,128)(2,1)}, u32[]{:S(2)}) copy-start(bf16[2048,256]{0,1:T(8,128)(2,1)} %get-tuple-element.27) | copy-start | bytes 3145732
  156.3 9.1 %copy-start.5 = (bf16[512,256]{0,1:T(8,128)(2,1)S(1)}, bf16[512,256]{0,1:T(8,128)(2,1)}, u32[]{:S(2)}) copy-start(bf16[512,256]{0,1:T(8,128)(2,1)} %copy.134) | copy-start | bytes 786436
  156.3 9.1 %copy-start.7 = (bf16[256,256]{0,1:T(8,128)(2,1)S(1)}, bf16[256,256]{0,1:T(8,128)(2,1)}, u32[]{:S(2)}) copy-start(bf16[256,256]{0,1:T(8,128)(2,1)} %copy.135) | copy-start | bytes 393220
  165.4 1.4 copy-start.3
  174.5 1.8 copy-start.9
Sparse Core Ops, SparseCore 0:
  20.8 18.0 all-gather.1
  176.4 23.4 reduce-scatter.1
where the time goes:
time: 208 us; the launch traced here: 207 us
  blocking collectives  56.8 us (27%)
  waiting for transfers between devices  45.1 us (22%)
  other arithmetic  31.6 us (15%)
  matrix products  24.6 us (12%)
  local copies, waits for them, and re-layouts  22.5 us (11%)
  between operations  14.4 us (7%)
  starting transfers between devices  11.7 us (6%)
    all_gather x1, blocking collectives, body(): root_values = lax.all_gather(prefix_root_values, 'dp', axis=0, tiled=True)  29.8 us
    all_gather x1, blocking collectives, body(): root_keys = lax.all_gather(prefix_root_keys, 'dp', axis=0, tiled=True)  27.1 us
    reduce_scatter x1, waiting for transfers between devices, body(): lax.psum_scatter(jnp.dot(attn, w_out, preferred_element_type=jnp.float32)...  22.7 us
    all_to_all x1, waiting for transfers between devices, body(): got = lax.all_to_all(sent, 'dp', split_axis=0, concat_axis=0, tiled=True)  22.3 us
    dot_general x1, matrix products, body(): jnp.einsum('tkgd,skd->kgts', heads_query, all_keys, preferred_element_typ...  10.1 us
    reduce_sum x1, other arithmetic, body(): total = jnp.sum(weights, axis=-1)  9.09 us
    dot_general x1, matrix products, body(): jnp.einsum('kgts,skd->kgtd', weights.astype(jnp.bfloat16), all_values, pr...  7.7 us
    all_to_all x1, starting transfers between devices, body(): lax.all_to_all(block_slot[:, None], 'dp', split_axis=0, concat_axis=0, ti...  7.28 us
  transfers between devices with their start and end apart: 4, of which 2 were waited for; matrix products, arithmetic and copies ran while one was open for 20% of the time, Pallas kernels for 0%

commit v1 on v0

--- a/solution.py
+++ b/solution.py
@@ -102,8 +102,16 @@
     )
     new_values = mixed[:, query_width + key_width :].astype(jnp.bfloat16)
     heads_query = query_matrix.reshape(height, kv_heads, query_group, head_dim)
-    root_keys = lax.all_gather(prefix_root_keys, "dp", axis=0, tiled=True)
-    root_values = lax.all_gather(prefix_root_values, "dp", axis=0, tiled=True)
+    root_keys, root_values = jnp.split(
+        lax.all_gather(
+            jnp.concatenate([prefix_root_keys, prefix_root_values], axis=1),
+            "dp",
+            axis=0,
+            tiled=True,
+        ),
+        [prefix_root_keys.shape[1]],
+        axis=1,
+    )
     owner_of = branch_nodes // MID_DEV
     owner_ids = jnp.arange(dp_count, dtype=jnp.int32)
     owner_match = owner_of[None, :] == owner_ids[:, None]

time: 208 us -> 171 us (0.82)
  blocking collectives: 56.8 us -> 0 us
  waiting for transfers between devices: 45.1 us -> 63.2 us
  other arithmetic: 31.6 us -> 36.6 us
  local copies, waits for them, and re-layouts: 22.5 us -> 18.6 us
    all_gather x2 -> x0, blocking collectives: 56.8 us -> none  [the longest x1 29.8 us: body(): root_values = lax.all_gather(prefix_root_values, 'dp', axis=0, tiled=True)]
    all_gather x0 -> x1, waiting for transfers between devices: none -> 36.3 us  [body(): lax.all_gather(jnp.concatenate([prefix_root_keys, prefix_root_values], ax...]
    all_to_all x1, waiting for transfers between devices: 22.3 us -> 2.8 us  [body(): got = lax.all_to_all(sent, 'dp', split_axis=0, concat_axis=0, tiled=True)]
    slice x3, local copies, waits for them, and re-layouts: 4.43 us -> 0.3 us  [body(): sent = jnp.where(second, own_pairs[1][None], own_pairs[0][None])]
    unnamed x33 -> x37, local copies, waits for them, and re-layouts: 6.52 us -> 5.72 us
  transfers between devices with their start and end apart: 4 -> 5, of which waited for: 2 -> 3; matrix products, arithmetic and copies ran while one was open for 20% -> 25% of each run, Pallas kernels for 0% -> 0%
where the time goes in v1:
time: 171 us
  waiting for transfers between devices  63.2 us (37%)
  other arithmetic  36.6 us (21%)
  matrix products  24.6 us (14%)
  local copies, waits for them, and re-layouts  18.6 us (11%)
  between operations  14.1 us (8%)
  starting transfers between devices  13.5 us (8%)
    all_gather x1, waiting for transfers between devices, body(): lax.all_gather(jnp.concatenate([prefix_root_keys, prefix_root_values], ax...  36.3 us
    reduce_scatter x1, waiting for transfers between devices, body(): lax.psum_scatter(jnp.dot(attn, w_out, preferred_element_type=jnp.float32)...  24 us
    dot_general x1, matrix products, body(): jnp.einsum('tkgd,skd->kgts', heads_query, all_keys, preferred_element_typ...  10.1 us
    reduce_sum x1, other arithmetic, body(): total = jnp.sum(weights, axis=-1)  9.09 us
    dot_general x1, matrix products, body(): jnp.einsum('kgts,skd->kgtd', weights.astype(jnp.bfloat16), all_values, pr...  7.7 us
    all_to_all x1, starting transfers between devices, body(): lax.all_to_all(block_slot[:, None], 'dp', split_axis=0, concat_axis=0, ti...  7.28 us
    concatenate x1, other arithmetic, body(): jnp.concatenate([jnp.ones((height, root_keys.shape[0]), jnp.bool_), leaf_...  6.99 us
    all_to_all x1, starting transfers between devices, body(): got = lax.all_to_all(sent, 'dp', split_axis=0, concat_axis=0, tiled=True)  6.11 us
  transfers between devices with their start and end apart: 5, of which 3 were waited for; matrix products, arithmetic and copies ran while one was open for 25% of the time, Pallas kernels for 0%

profile of v1, /device:TPU:0, one launch (start us, length us, event | category | flops | bytes accessed | tf_op | source)
XLA Modules:
  0.0 170.7 jit_solution(8407628438155703135)
XLA Ops:
  9.2 1.8 %fusion.24 = bf16[64,2048]{1,0:T(8,128)(2,1)} fusion(bf16[64,2048]{1,0:T(8,128)(2,1)} %param.18, f32[2048]{0:T(1024)S(1)} %convert_element_type.58, f32[64]{0:T(128)S(1)} %add_rsqrt_fusion.2), kind=kLoop, calls=%fused_computation.28 | loop fusion | flops 524288 | bytes 532736 | tf_op jit(solution)/shard_map/convert_element_type | solution.py:63
  13.4 7.3 %all-to-all-start = ((s32[8,1,1]{2,1,0:T(1,128)}), s32[8,1,1]{2,1,0:T(1,128)S(1)}, u32[]{:S(2)}, u32[]{:S(2)}) async-start(s32[8,1,1]{2,1,0:T(1,128)} %copy.123), calls=%async_computation | async-start | bytes 8192 | tf_op jit(solution)/shard_map/all_to_all | solution.py:121
  24.6 1.2 add.74
  25.8 1.5 fusion.28
  27.3 1.3 convert_reduce_fusion
  32.5 1.3 select_reduce_fusion.3
  37.2 1.1 multiply_cosine_fusion
  38.6 1.6 broadcast_select_fusion
  40.1 6.1 %all-to-all-start.1 = ((bf16[8,256,512]{1,2,0:T(8,128)(2,1)}), bf16[8,256,512]{1,2,0:T(8,128)(2,1)}, u32[]{:S(2)}, u32[]{:S(2)}) async-start(bf16[8,256,512]{1,2,0:T(8,128)(2,1)} %broadcast_select_fusion), calls=%async_computation.1 | async-start | bytes 4194304 | tf_op jit(solution)/shard_map/all_to_all | solution.py:129
  46.3 7.0 %pad_add_fusion = pred[256,3840]{0,1:T(8,128)(4,1)} fusion(pred[256,2048]{0,1:T(8,128)(4,1)S(1)} %broadcast_compare_fusion, pred[256,256]{0,1:T(8,128)(4,1)S(1)} %copy-done.12, pred[256,512]{0,1:T(8,128)(4,1)S(1)} %broadcast_compare_fusion.1, pred[3840]{0:T(1024)(128)(4,1)S(1)} %pad.8.clone), kind=kLoop, calls=%fused_computation.7 | loop fusion | flops 2949120 | bytes 1707776 | tf_op jit(solution)/shard_map/concatenate | solution.py:137
  53.3 2.0 %convolution_convert_fusion.1 = bf16[256,256]{1,0:T(8,128)(2,1)S(1)} fusion(bf16[256,2048]{1,0:T(8,128)(2,1)} %all-gather.5.cloned.1.call-done, bf16[2048,256]{1,0:T(8,128)(2,1)} %param.22), kind=kOutput, calls=%fused_computation.20 | convolution fusion | flops 268500992 | bytes 2228224 | tf_op jit(solution)/shard_map/dot_general | solution.py:69
  56.1 2.6 %fusion.37 = f32[256,512]{1,0:T(8,128)S(1)} fusion(bf16[256,2048]{1,0:T(8,128)(2,1)} %all-gather.5.cloned.1.call-done, bf16[2048,512]{1,0:T(8,128)(2,1)} %param.20), kind=kOutput, calls=%fused_computation.84 | convolution fusion | flops 536870912 | bytes 3670016 | tf_op jit(solution)/shard_map/dot_general | solution.py:67
  62.8 36.3 %all-gather.3.cloned.1.call-done = bf16[1024,512]{0,1:T(8,128)(2,1)} async-done(((bf16[128,512]{0,1:T(8,128)(2,1)}), bf16[1024,512]{0,1:T(8,128)(2,1)}) %all-gather.3.cloned.1.call-update) | async-done | bytes 1048592 | tf_op jit(solution)/shard_map/all_gather | solution.py:106
  99.1 2.1 %fusion.35 = (bf16[1024,256]{0,1:T(8,128)(2,1)S(1)}, bf16[1024,256]{0,1:T(8,128)(2,1)}) fusion(bf16[1024,512]{0,1:T(8,128)(2,1)} %all-gather.3.cloned.1.call-done), kind=kLoop, calls=%fused_computation.82 | loop fusion | bytes 2097152 | tf_op jit(solution)/shard_map/split | solution.py:105
  102.1 2.8 %all-to-all-done.1 = bf16[8,256,512]{1,2,0:T(8,128)(2,1)} async-done(((bf16[8,256,512]{1,2,0:T(8,128)(2,1)}), bf16[8,256,512]{1,2,0:T(8,128)(2,1)}, u32[]{:S(2)}, u32[]{:S(2)}) %all-to-all-start.1) | async-done | bytes 2097184 | tf_op jit(solution)/shard_map/all_to_all | solution.py:129
  104.9 1.9 %copy.142 = bf16[8,64,8,256]{3,2,0,1:T(8,128)(2,1)S(1)} copy(bf16[8,64,8,256]{3,2,1,0:T(8,128)(2,1)} %bitcast.24) | data formatting | bytes 4194304 | tf_op jit(solution)/shard_map/reshape | solution.py:130
  106.8 1.1 fusion.34
  107.9 1.3 copy.129
  109.3 10.1 %fusion.2 = (f32[2,2,256]{2,1,0:T(2,128)S(1)}, f32[2,3840,256,2]{2,1,3,0:T(8,128)}) fusion(pred[256,3840]{0,1:T(8,128)(4,1)} %pad_add_fusion, bf16[256,2,2,64]{3,0,2,1:T(8,128)(2,1)} %bitcast.71, bf16[256,2,2,64]{3,0,2,1:T(8,128)(2,1)} %bitcast.72, bf16[2048,2,128]{2,0,1:T(8,128)(2,1)} %copy.129, bf16[256,2,128]{2,0,1:T(8,128)(2,1)S(1)} %maximum_convert_fusion, ...), kind=kOutput, calls=%fused_computation.4 | convolution fusion | flops 1026817024 | bytes 18944000 | tf_op jit(solution)/shard_map/tkgd,skd->kgts/dot_general | solution.py:152
  119.3 9.1 %fusion = f32[2,2,256]{2,1,0:T(2,128)S(1)} fusion(f32[2,3840,256,2]{2,1,3,0:T(8,128)} %get-tuple-element.43, f32[2,2,256]{2,1,0:T(2,128)S(1)} %get-tuple-element.42, pred[256,3840]{0,1:T(8,128)(4,1)} %pad_add_fusion), kind=kLoop, calls=%fused_computation.2 | loop fusion | flops 15727616 | bytes 16719872 | tf_op jit(solution)/shard_map/reduce_sum | solution.py:155
  128.5 1.2 pad_maximum_fusion
  129.8 7.7 %fusion.19 = bf16[256,2,2,128]{0,3,2,1:T(8,128)(2,1)S(1)} fusion(bf16[3840,2,128,1]{0,2,3,1:T(8,128)(2,1)S(1)} %bitcast.67, f32[2,3840,256,2]{2,1,3,0:T(8,128)} %get-tuple-element.43, f32[2,2,256]{2,1,0:T(2,128)S(1)} %get-tuple-element.42, pred[256,3840]{0,1:T(8,128)(4,1)S(1)} %copy-done.3, f32[256,2,2]{0,2,1:T(2,128)S(1)} %bitcast.80), kind=kOutput, calls=%fused_computation.22 | convolution fusion | flops 1022623744 | bytes 18948096 | tf_op jit(solution)/shard_map/kgts,skd->kgtd/dot_general | solution.py:156
  137.5 1.7 %convolution_convert_fusion = bf16[256,2048]{1,0:T(8,128)(2,1)} fusion(bf16[256,512]{0,1:T(8,128)(2,1)S(1)} %bitcast.73, bf16[512,2048]{1,0:T(8,128)(2,1)S(1)} %copy-done), kind=kOutput, calls=%fused_computation.8 | convolution fusion | flops 537395200 | bytes 3407872 | tf_op jit(solution)/shard_map/dot_general | solution.py:165
  140.1 24.0 %reduce-scatter.2.cloned.1.call-done = bf16[64,2048]{1,0:T(8,128)(2,1)} async-done(((bf16[256,2048]{1,0:T(8,128)(2,1)}), bf16[64,2048]{1,0:T(8,128)(2,1)}) %reduce-scatter.2.cloned.1.call-update) | async-done | bytes 262160 | tf_op jit(solution)/shard_map/reduce_scatter | solution.py:164
  (87 shorter events, 22.5 us)
Async XLA Ops:
  7.2 130.3 %copy-start = (bf16[512,2048]{1,0:T(8,128)(2,1)S(1)}, bf16[512,2048]{1,0:T(8,128)(2,1)}, u32[]{:S(2)}) copy-start(bf16[512,2048]{1,0:T(8,128)(2,1)} %param.25) | copy-start | bytes 6291460
  7.2 24.6 %copy-start.13 = (s32[1,256]{1,0:T(1,128)S(1)}, s32[1,256]{1,0:T(1,128)}, u32[]{:S(2)}) copy-start(s32[1,256]{1,0:T(1,128)} %param.34) | copy-start | bytes 3076
  7.2 23.6 %copy-start.10 = (bf16[512,256]{1,0:T(8,128)(2,1)S(1)}, bf16[512,256]{1,0:T(8,128)(2,1)}, u32[]{:S(2)}) copy-start(bf16[512,256]{1,0:T(8,128)(2,1)} %param.32) | copy-start | bytes 786436
  7.2 25.3 %copy-start.14 = (bf16[128]{0:T(256)(128)(2,1)S(1)}, bf16[128]{0:T(256)(128)(2,1)}, u32[]{:S(2)}) copy-start(bf16[128]{0:T(256)(128)(2,1)} %param.23) | copy-start | bytes 772
  7.2 46.1 %all-gather.5.cloned.1.call-start = ((), (), s32[]{:S(2)}) async-start(), calls=%async_computation.4 | async-start | bytes 1310720 | tf_op jit(solution)/shard_map/all_gather | solution.py:64
  13.4 24.9 %all-to-all-start = ((s32[8,1,1]{2,1,0:T(1,128)}), s32[8,1,1]{2,1,0:T(1,128)S(1)}, u32[]{:S(2)}, u32[]{:S(2)}) async-start(s32[8,1,1]{2,1,0:T(1,128)} %copy.123), calls=%async_computation | async-start | bytes 8192 | tf_op jit(solution)/shard_map/all_to_all | solution.py:121
  20.7 78.4 %all-gather.3.cloned.1.call-start = ((), (), s32[]{:S(2)}) async-start(), calls=%async_computation.3 | async-start | bytes 1179648 | tf_op jit(solution)/shard_map/all_gather | solution.py:106
  40.1 6.2 %copy-start.12 = (pred[256,256]{0,1:T(8,128)(4,1)S(1)}, pred[256,256]{0,1:T(8,128)(4,1)}, u32[]{:S(2)}) copy-start(pred[256,256]{0,1:T(8,128)(4,1)} %fusion.28) | copy-start | bytes 196612
  40.1 64.8 %all-to-all-start.1 = ((bf16[8,256,512]{1,2,0:T(8,128)(2,1)}), bf16[8,256,512]{1,2,0:T(8,128)(2,1)}, u32[]{:S(2)}, u32[]{:S(2)}) async-start(bf16[8,256,512]{1,2,0:T(8,128)(2,1)} %broadcast_select_fusion), calls=%async_computation.1 | async-start | bytes 4194304 | tf_op jit(solution)/shard_map/all_to_all | solution.py:129
  46.3 117.9 %reduce-scatter.2.cloned.1.call-start = ((), (), s32[]{:S(2)}) async-start(), calls=%async_computation.5 | async-start | bytes 1310720 | tf_op jit(solution)/shard_map/reduce_scatter | solution.py:164
  55.3 4.9 %copy-start.6 = (bf16[256,256]{1,0:T(8,128)(2,1)}, bf16[256,256]{1,0:T(8,128)(2,1)S(1)}, u32[]{:S(2)}) copy-start(bf16[256,256]{1,0:T(8,128)(2,1)S(1)} %convolution_convert_fusion.1) | copy-start | bytes 393220
  58.9 2.8 %copy-start.1 = (bf16[256,2048]{1,0:T(8,128)(2,1)S(1)}, bf16[256,2048]{1,0:T(8,128)(2,1)}, u32[]{:S(2)}) copy-start(bf16[256,2048]{1,0:T(8,128)(2,1)} %all-gather.5.cloned.1.call-done) | copy-start | bytes 3145732
  58.9 2.8 %copy-start.4 = (bf16[2048,256]{1,0:T(8,128)(2,1)S(1)}, bf16[2048,256]{1,0:T(8,128)(2,1)}, u32[]{:S(2)}) copy-start(bf16[2048,256]{1,0:T(8,128)(2,1)} %param.21) | copy-start | bytes 3145732
  62.8 46.5 %copy-start.8 = (bf16[256,2,128]{2,0,1:T(8,128)(2,1)}, bf16[256,2,128]{2,0,1:T(8,128)(2,1)S(1)}, u32[]{:S(2)}) copy-start(bf16[256,2,128]{2,0,1:T(8,128)(2,1)S(1)} %maximum_convert_fusion) | copy-start | bytes 393220
  106.8 2.5 %copy-start.11 = (bf16[512,2,128]{2,0,1:T(8,128)(2,1)S(1)}, bf16[512,2,128]{2,0,1:T(8,128)(2,1)}, u32[]{:S(2)}) copy-start(bf16[512,2,128]{2,0,1:T(8,128)(2,1)} %copy.128) | copy-start | bytes 786436
  119.3 9.1 %copy-start.2 = (bf16[2048,256]{0,1:T(8,128)(2,1)S(1)}, bf16[2048,256]{0,1:T(8,128)(2,1)}, u32[]{:S(2)}) copy-start(bf16[2048,256]{0,1:T(8,128)(2,1)} %get-tuple-element.27) | copy-start | bytes 3145732
  119.3 9.1 %copy-start.5 = (bf16[512,256]{0,1:T(8,128)(2,1)S(1)}, bf16[512,256]{0,1:T(8,128)(2,1)}, u32[]{:S(2)}) copy-start(bf16[512,256]{0,1:T(8,128)(2,1)} %copy.134) | copy-start | bytes 786436
  119.3 9.1 %copy-start.7 = (bf16[256,256]{0,1:T(8,128)(2,1)S(1)}, bf16[256,256]{0,1:T(8,128)(2,1)}, u32[]{:S(2)}) copy-start(bf16[256,256]{0,1:T(8,128)(2,1)} %copy.135) | copy-start | bytes 393220
  128.4 1.4 copy-start.3
  137.5 1.8 %copy-start.9 = (bf16[256,2,128]{2,0,1:T(8,128)(2,1)S(1)}, bf16[256,2,128]{2,0,1:T(8,128)(2,1)}, u32[]{:S(2)}) copy-start(bf16[256,2,128]{2,0,1:T(8,128)(2,1)} %copy-done.8) | copy-start | bytes 393220
Sparse Core Ops, SparseCore 0:
  11.2 19.4 all-gather.4
  32.7 66.3 all-gather.2
  139.4 24.7 reduce-scatter.1
